TPU v7x, 256 devices: a whole 4x4x8 slice. The times are simulated.
256 devices in a mesh: seq: 16 (over z, x_lo), wt: 16 (over x_hi, y, core).
Axes of the slice: x: 4 (x_hi: 2, x_lo: 2; x = x_hi * 2 + x_lo), y: 4, z: 8, core: 2. Of those that a mesh axis runs over, the one named last changes fastest.
Arguments:
- frames: bfloat16 [4096, 4096], P('seq'), may hold values from -40 to 40
- attn_norm_gain: float32 [4096], replicated, may hold values from 0.1 to 1.9
- qkv_weight: bfloat16 [3, 4096, 4096], P(None, 'seq', 'wt'), may hold values from -4 to 4
- attn_out_weight: bfloat16 [4096, 4096], P('seq', 'wt'), may hold values from -0.125 to 0.125
- conv_norm_gain: float32 [4096], replicated, may hold values from 0.1 to 1.9
- glu_weight: bfloat16 [2, 4096, 4096], P(None, 'seq', 'wt'), may hold values from -0.09375 to 0.09375
- depth_kernel: float32 [31, 4096], P(None, 'wt'), may hold values from -1 to 1
- norm_scale: float32 [4096], P('wt'), may hold values from 0.5 to 2
- norm_shift: float32 [4096], P('wt'), may hold values from -3 to 3
- conv_out_weight: bfloat16 [4096, 4096], P('seq', 'wt'), may hold values from -0.125 to 0.125
Outputs:
- encoded: bfloat16 [4096, 4096], P('seq', 'wt')
All inputs are finite; a program needn't handle non-finite values.
Results may differ from a plain program's by a relative error of at most 0.014.
Values may be sent and summed in bfloat16 or wider, within the bound.
No kernel may reach another device: no remote copies, remote signals or barrier semaphores. Data moves between devices by JAX's collectives and lax.ppermute only.
A program may use at most 64 MiB of HBM per device.

v0:
```python
import jax
import jax.numpy as jnp
from jax import lax
from jax.sharding import PartitionSpec as P

HEAD_DIM = 128


def padded_2(value, sides, width):
    for axis, dim in sides:
        devices, length = (lax.axis_size(axis), value.shape[dim])
        up = [(i, (i + 1) % devices) for i in range(devices - 1)]
        down = [(j, i) for i, j in up]
        last = lax.slice_in_dim(value, length - width, length, axis=dim)
        first = lax.slice_in_dim(value, 0, width, axis=dim)
        before = lax.ppermute(last, axis, up)
        after = lax.ppermute(first, axis, down)
        value = jnp.concatenate([before, value, after], axis=dim)
    return value


def norm_rows(values, gain_vec):
    wide = values.astype(jnp.float32)
    row_mean = jnp.mean(wide, axis=-1, keepdims=True)
    centered = wide - row_mean
    row_var = jnp.mean(centered * centered, axis=-1, keepdims=True)
    return (centered * lax.rsqrt(row_var + 1e-05) * gain_vec).astype(jnp.bfloat16)


def project_in(normed, stacked):
    return jnp.einsum(
        "rd,mdc->rmc",
        normed,
        lax.all_gather(stacked, "seq", axis=1, tiled=True),
        preferred_element_type=jnp.float32,
    )


def project_out(inputs, weight):
    return lax.dot_general(
        inputs,
        lax.all_gather(weight, "seq", axis=0, tiled=True),
        (((1,), (1,)), ((), ())),
        preferred_element_type=jnp.float32,
    )


def feature_share(partial_sums):
    return lax.psum_scatter(
        partial_sums.astype(jnp.bfloat16), "wt", scatter_dimension=1, tiled=True
    ).astype(jnp.float32)


def local(
    frames,
    attn_norm_gain,
    qkv_weight,
    attn_out_weight,
    conv_norm_gain,
    glu_weight,
    depth_kernel,
    norm_scale,
    norm_shift,
    conv_out_weight,
):
    row_count = frames.shape[0]
    col_count = qkv_weight.shape[2]
    heads_here = col_count // HEAD_DIM
    column_start = lax.axis_index("wt") * col_count
    normed = norm_rows(frames, attn_norm_gain)
    projected = project_in(normed, qkv_weight).astype(jnp.bfloat16)
    query_heads = projected[:, 0].reshape(row_count, heads_here, HEAD_DIM)
    keys = projected[:, 1]
    values = projected[:, 2]
    score_scale = HEAD_DIM ** (-0.5)
    key_segment = lax.all_gather(keys, "seq", axis=0, tiled=True)
    value_segment = lax.all_gather(values, "seq", axis=0, tiled=True)
    row_best = jnp.full((heads_here, row_count), -1e30, jnp.float32)
    key_heads = key_segment.reshape(key_segment.shape[0], heads_here, HEAD_DIM)
    value_heads = value_segment.reshape(value_segment.shape[0], heads_here, HEAD_DIM)
    scores = (
        jnp.einsum("qhd,khd->hqk", query_heads, key_heads, preferred_element_type=jnp.float32)
        * score_scale
    )
    new_best = jnp.maximum(row_best, jnp.max(scores, axis=-1))
    exp_weights = jnp.exp(scores - new_best[..., None])
    running_sum = jnp.sum(exp_weights, axis=-1)
    weighted = jnp.einsum(
        "hqk,khd->hqd",
        exp_weights.astype(jnp.bfloat16),
        value_heads,
        preferred_element_type=jnp.float32,
    )
    row_best, running_sum, weighted = (new_best, running_sum, weighted)
    context = (
        (weighted / running_sum[..., None])
        .transpose(1, 0, 2)
        .reshape(row_count, col_count)
        .astype(jnp.bfloat16)
    )
    attended = project_out(context, attn_out_weight)
    share_cols = feature_share(attended)
    frame_cols = lax.dynamic_slice_in_dim(frames, column_start, col_count, 1)
    residual_cols = (frame_cols.astype(jnp.float32) + share_cols).astype(jnp.bfloat16)
    residual_full = lax.all_gather(residual_cols, "wt", axis=1, tiled=True)
    normed_conv = norm_rows(residual_full, conv_norm_gain)
    glu_pair = project_in(normed_conv, glu_weight)
    gated = (glu_pair[:, 0] * jax.nn.sigmoid(glu_pair[:, 1])).astype(jnp.bfloat16)
    rim_width = (depth_kernel.shape[0] - 1) // 2
    padded = padded_2(gated, (("seq", 0),), rim_width).astype(jnp.float32)
    depth_out = jnp.zeros((row_count, col_count), jnp.float32)
    for tap_index in range(depth_kernel.shape[0]):
        depth_out = depth_out + depth_kernel[tap_index] * padded[tap_index : tap_index + row_count]
    shifted = depth_out * norm_scale + norm_shift
    activated = (shifted * jax.nn.sigmoid(shifted)).astype(jnp.bfloat16)
    conv_cols = feature_share(project_out(activated, conv_out_weight))
    residual_cols = lax.dynamic_slice_in_dim(residual_full, column_start, col_count, 1)
    return (residual_cols.astype(jnp.float32) + conv_cols).astype(jnp.bfloat16)


def solution(mesh):
    in_specs = (
        P("seq", None),
        P(),
        P(None, "seq", "wt"),
        P("seq", "wt"),
        P(),
        P(None, "seq", "wt"),
        P(None, "wt"),
        P("wt"),
        P("wt"),
        P("seq", "wt"),
    )
    out_specs = P("seq", "wt")
    return jax.shard_map(local, mesh=mesh, in_specs=in_specs, out_specs=out_specs, check_vma=False)
```

profile of v0, /device:TPU:32, one launch (start us, length us, event | category | flops | bytes accessed | tf_op | source)
XLA Modules:
  0.0 819.5 jit_solution(16398674720940230616)
XLA Ops:
  6.5 2.1 copy.11
  8.6 0.0 all-gather.10.cloned.1.call-update
  8.6 0.0 all-gather.20.cloned.1.call-start
  8.7 2.0 convert_reduce_fusion.1
  10.7 0.7 fusion.9
  11.4 156.5 %all-gather.10.cloned.1.call-done = bf16[3,4096,256]{1,2,0:T(8,128)(2,1)} async-done(((bf16[3,256,256]{1,2,0:T(8,128)(2,1)}), bf16[3,4096,256]{1,2,0:T(8,128)(2,1)}) %all-gather.10.cloned.1.call-update) | async-done | bytes 6291472 | tf_op jit(solution)/shard_map/all_gather | solution.py:34
  167.9 4.7 fusion.28
  172.6 0.7 fusion.113
  173.3 0.0 all-gather.20.cloned.1.call-update
  173.4 0.0 all-gather.22.cloned.1.call-start
  173.4 0.7 all-gather.22.cloned.1.call-update
  174.1 0.0 all-gather.12.cloned.1.call-start
  174.1 0.5 all-gather.12.cloned.1.call-update
  174.7 0.0 reduce-scatter.3.cloned.1.call-start
  174.7 85.2 %all-gather.20.cloned.1.call-done = bf16[4096,1,256]{0,2,1:T(8,128)(2,1)} async-done(((bf16[256,1,256]{0,2,1:T(8,128)(2,1)}), bf16[4096,1,256]{0,2,1:T(8,128)(2,1)}) %all-gather.20.cloned.1.call-update) | async-done | bytes 2097168 | tf_op jit(solution)/shard_map/all_gather | solution.py:76
  260.0 3.0 multiply_reduce_fusion
  263.0 3.2 copy-done
  266.2 1.5 fusion
  267.7 77.6 %all-gather.22.cloned.1.call-done = bf16[4096,1,256]{0,2,1:T(8,128)(2,1)} async-done(((bf16[256,1,256]{0,2,1:T(8,128)(2,1)}), bf16[4096,1,256]{0,2,1:T(8,128)(2,1)}) %all-gather.22.cloned.1.call-update) | async-done | bytes 2097168 | tf_op jit(solution)/shard_map/all_gather | solution.py:77
  345.3 5.8 fusion.37
  351.1 0.0 copy-start.3
  351.1 69.0 %all-gather.12.cloned.1.call-done = bf16[4096,256]{1,0:T(8,128)(2,1)} async-done(((bf16[256,256]{1,0:T(8,128)(2,1)}), bf16[4096,256]{1,0:T(8,128)(2,1)}) %all-gather.12.cloned.1.call-update) | async-done | bytes 2097168 | tf_op jit(solution)/shard_map/all_gather | solution.py:42
  420.2 3.7 convolution_convert_fusion.1
  423.9 0.0 reduce-scatter.3.cloned.1.call-update
  423.9 0.0 all-gather.14.cloned.1.call-start
  423.9 77.6 %reduce-scatter.3.cloned.1.call-done = bf16[256,256]{1,0:T(8,128)(2,1)} async-done(((bf16[256,4096]{1,0:T(8,128)(2,1)}), bf16[256,256]{1,0:T(8,128)(2,1)}) %reduce-scatter.3.cloned.1.call-update) | async-done | bytes 131088 | tf_op jit(solution)/shard_map/reduce_scatter | solution.py:49
  501.5 1.6 add_convert_fusion.1
  503.1 0.0 all-gather.14.cloned.1.call-update
  503.1 0.0 all-gather.16.cloned.1.call-start
  503.2 0.7 all-gather.16.cloned.1.call-update
  503.9 0.0 all-gather.18.cloned.1.call-start
  503.9 0.7 all-gather.18.cloned.1.call-update
  504.6 0.0 reduce-scatter.5.cloned.1.call-start
  504.7 50.7 %all-gather.14.cloned.1.call-done = bf16[256,4096]{1,0:T(8,128)(2,1)} async-done(((bf16[256,256]{1,0:T(8,128)(2,1)}), bf16[256,4096]{1,0:T(8,128)(2,1)}) %all-gather.14.cloned.1.call-update) | async-done | bytes 2097168 | tf_op jit(solution)/shard_map/all_gather | solution.py:105
  555.5 2.1 convert_reduce_fusion
  557.6 2.3 fusion.6
  559.9 94.7 %all-gather.16.cloned.1.call-done = bf16[2,4096,256]{2,1,0:T(8,128)(2,1)} async-done(((bf16[2,256,256]{2,1,0:T(8,128)(2,1)}), bf16[2,4096,256]{2,1,0:T(8,128)(2,1)}) %all-gather.16.cloned.1.call-update) | async-done | bytes 4194320 | tf_op jit(solution)/shard_map/all_gather | solution.py:34
  654.6 3.5 fusion.20
  658.1 0.1 fusion.76
  658.2 3.9 collective-permute-start
  662.0 2.9 collective-permute-start.1
  664.9 0.1 fusion.124
  665.0 2.6 collective-permute-done.1
  667.6 61.0 %all-gather.18.cloned.1.call-done = bf16[4096,256]{1,0:T(8,128)(2,1)} async-done(((bf16[256,256]{1,0:T(8,128)(2,1)}), bf16[4096,256]{1,0:T(8,128)(2,1)}) %all-gather.18.cloned.1.call-update) | async-done | bytes 2097168 | tf_op jit(solution)/shard_map/all_gather | solution.py:42
  728.6 4.6 convolution_convert_fusion
  733.2 0.0 reduce-scatter.5.cloned.1.call-update
  733.2 78.1 %reduce-scatter.5.cloned.1.call-done = bf16[256,256]{1,0:T(8,128)(2,1)} async-done(((bf16[256,4096]{1,0:T(8,128)(2,1)}), bf16[256,256]{1,0:T(8,128)(2,1)}) %reduce-scatter.5.cloned.1.call-update) | async-done | bytes 131088 | tf_op jit(solution)/shard_map/reduce_scatter | solution.py:49
  811.3 1.6 add_convert_fusion
  (25 shorter events, 0.1 us)
Async XLA Ops:
  6.5 4.1 copy-start.1
  6.5 161.3 %copy-start.4 = (f32[4096]{0:T(1024)S(1)}, f32[4096]{0:T(1024)}, u32[]{:S(2)}) copy-start(f32[4096]{0:T(1024)} %param.11) | copy-start | bytes 49156
  6.5 161.3 %all-gather.10.cloned.1.call-start = ((), (), s32[]{:S(2)}) async-start(), calls=%async_computation.2 | async-start | bytes 6684672 | tf_op jit(solution)/shard_map/all_gather | solution.py:34
  8.6 251.3 %all-gather.20.cloned.1.call-start = ((), (), s32[]{:S(2)}) async-start(), calls=%async_computation.9 | async-start | bytes 2228224 | tf_op jit(solution)/shard_map/all_gather | solution.py:76
  173.4 172.0 %all-gather.22.cloned.1.call-start = ((), (), s32[]{:S(2)}) async-start(), calls=%async_computation.10 | async-start | bytes 2228224 | tf_op jit(solution)/shard_map/all_gather | solution.py:77
  174.1 246.1 %all-gather.12.cloned.1.call-start = ((), (), s32[]{:S(2)}) async-start(), calls=%async_computation.3 | async-start | bytes 2228224 | tf_op jit(solution)/shard_map/all_gather | solution.py:42
  174.7 326.9 %reduce-scatter.3.cloned.1.call-start = ((), (), s32[]{:S(2)}) async-start(), calls=%async_computation.4 | async-start | bytes 2228224 | tf_op jit(solution)/shard_map/reduce_scatter | solution.py:49
  262.9 3.2 copy-start
  351.1 153.6 %copy-start.3 = (f32[31,256]{1,0:T(8,128)S(1)}, f32[31,256]{1,0:T(8,128)}, u32[]{:S(2)}) copy-start(f32[31,256]{1,0:T(8,128)} %param.16) | copy-start | bytes 95236
  423.9 230.7 %copy-start.5 = (f32[4096]{0:T(1024)S(1)}, f32[4096]{0:T(1024)}, u32[]{:S(2)}) copy-start(f32[4096]{0:T(1024)} %param.14) | copy-start | bytes 49156
  423.9 131.6 %all-gather.14.cloned.1.call-start = ((), (), s32[]{:S(2)}) async-start(), calls=%async_computation.5 | async-start | bytes 2228224 | tf_op jit(solution)/shard_map/all_gather | solution.py:105
  503.1 151.4 %all-gather.16.cloned.1.call-start = ((), (), s32[]{:S(2)}) async-start(), calls=%async_computation.6 | async-start | bytes 4456448 | tf_op jit(solution)/shard_map/all_gather | solution.py:34
  503.9 224.7 %all-gather.18.cloned.1.call-start = ((), (), s32[]{:S(2)}) async-start(), calls=%async_computation.7 | async-start | bytes 2228224 | tf_op jit(solution)/shard_map/all_gather | solution.py:42
  504.6 306.7 %reduce-scatter.5.cloned.1.call-start = ((), (), s32[]{:S(2)}) async-start(), calls=%async_computation.8 | async-start | bytes 2228224 | tf_op jit(solution)/shard_map/reduce_scatter | solution.py:49
  555.5 99.1 %copy-start.2 = (bf16[256,4096]{1,0:T(8,128)(2,1)S(1)}, bf16[256,4096]{1,0:T(8,128)(2,1)}, u32[]{:S(2)}) copy-start(bf16[256,4096]{1,0:T(8,128)(2,1)} %all-gather.14.cloned.1.call-done) | copy-start | bytes 6291460
  559.9 168.8 %copy-start.6 = (f32[256]{0:T(256)S(1)}, f32[256]{0:T(256)}, u32[]{:S(2)}) copy-start(f32[256]{0:T(256)} %param.18) | copy-start | bytes 3076
  559.9 168.7 %copy-start.7 = (f32[256]{0:T(256)S(1)}, f32[256]{0:T(256)}, u32[]{:S(2)}) copy-start(f32[256]{0:T(256)} %param.17) | copy-start | bytes 3076
  658.2 6.8 collective-permute-start
  662.0 5.5 collective-permute-start.1
Sparse Core Ops, SparseCore 0:
  9.1 158.7 all-gather.9
  173.5 86.4 all-gather.19
  261.7 83.6 all-gather.21
  347.0 73.1 all-gather.11
  424.2 77.2 reduce-scatter.2
  504.3 51.1 all-gather.13
  557.4 97.1 all-gather.15
  656.5 72.0 all-gather.17
  733.4 77.9 reduce-scatter.4
where the time goes:
time: 820 us; the launch traced here: 819 us
  waiting for transfers between devices  756 us (92%)
  matrix products  25.2 us (3%)
  between operations  13.4 us (2%)
  other arithmetic  11.9 us (1%)
    all_gather x2, waiting for transfers between devices, project_in(): lax.all_gather(stacked, 'seq', axis=1, tiled=True)  251 us
    reduce_scatter x2, waiting for transfers between devices, feature_share(): lax.psum_scatter(partial_sums.astype(jnp.bfloat16), 'wt', scatter_dimensi...  156 us
    all_gather x2, waiting for transfers between devices, project_out(): lax.all_gather(weight, 'seq', axis=0, tiled=True)  130 us
    all_gather x1, waiting for transfers between devices, local(): key_segment = lax.all_gather(keys, 'seq', axis=0, tiled=True)  85.2 us
    all_gather x1, waiting for transfers between devices, local(): value_segment = lax.all_gather(values, 'seq', axis=0, tiled=True)  77.6 us
    all_gather x1, waiting for transfers between devices, local(): residual_full = lax.all_gather(residual_cols, 'wt', axis=1, tiled=True)  50.7 us
  transfers between devices with their start and end apart: 11, of which 10 were waited for; matrix products, arithmetic and copies ran while one was open for 3% of the time, Pallas kernels for 0%

commit v1 on v0

--- a/solution.py
+++ b/solution.py
@@ -73,8 +73,11 @@
     keys = projected[:, 1]
     values = projected[:, 2]
     score_scale = HEAD_DIM ** (-0.5)
-    key_segment = lax.all_gather(keys, "seq", axis=0, tiled=True)
-    value_segment = lax.all_gather(values, "seq", axis=0, tiled=True)
+    key_segment, value_segment = jnp.split(
+        lax.all_gather(jnp.concatenate([keys, values], 1), axis_name="seq", axis=0, tiled=True),
+        [keys.shape[1]],
+        1,
+    )
     row_best = jnp.full((heads_here, row_count), -1e30, jnp.float32)
     key_heads = key_segment.reshape(key_segment.shape[0], heads_here, HEAD_DIM)
     value_heads = value_segment.reshape(value_segment.shape[0], heads_here, HEAD_DIM)

time: 820 us -> 772 us (0.941)
  waiting for transfers between devices: 756 us -> 713 us
    all_gather x2 -> x1, waiting for transfers between devices: 163 us -> 121 us  [local(): lax.all_gather(jnp.concatenate([keys, values], 1), axis_name='seq', axis=...]
  transfers between devices with their start and end apart: 11 -> 10, of which waited for: 10 -> 9; matrix products, arithmetic and copies ran while one was open for 3% -> 2% of each run, Pallas kernels for 0% -> 0%
where the time goes in v1:
time: 772 us; the launch traced here: 771 us
  waiting for transfers between devices  713 us (92%)
  matrix products  19.7 us (3%)
  between operations  13.7 us (2%)
  other arithmetic  12.7 us (2%)
    all_gather x2, waiting for transfers between devices, project_in(): lax.all_gather(stacked, 'seq', axis=1, tiled=True)  251 us
    reduce_scatter x2, waiting for transfers between devices, feature_share(): lax.psum_scatter(partial_sums.astype(jnp.bfloat16), 'wt', scatter_dimensi...  156 us
    all_gather x2, waiting for transfers between devices, project_out(): lax.all_gather(weight, 'seq', axis=0, tiled=True)  131 us
    all_gather x1, waiting for transfers between devices, local(): lax.all_gather(jnp.concatenate([keys, values], 1), axis_name='seq', axis=...  121 us
    all_gather x1, waiting for transfers between devices, local(): residual_full = lax.all_gather(residual_cols, 'wt', axis=1, tiled=True)  50.9 us
  transfers between devices with their start and end apart: 10, of which 9 were waited for; matrix products, arithmetic and copies ran while one was open for 2% of the time, Pallas kernels for 0%

profile of v1, /device:TPU:32, one launch (start us, length us, event | category | flops | bytes accessed | tf_op | source)
XLA Modules:
  0.0 771.5 jit_solution(17229595017992850027)
XLA Ops:
  6.5 2.1 copy.11
  8.6 0.0 all-gather.7.cloned.1.call-update
  8.6 0.0 all-gather.9.cloned.1.call-start
  8.7 2.0 convert_reduce_fusion.1
  10.7 0.7 fusion.9
  11.4 156.5 %all-gather.7.cloned.1.call-done = bf16[3,4096,256]{1,2,0:T(8,128)(2,1)} async-done(((bf16[3,256,256]{1,2,0:T(8,128)(2,1)}), bf16[3,4096,256]{1,2,0:T(8,128)(2,1)}) %all-gather.7.cloned.1.call-update) | async-done | bytes 6291472 | tf_op jit(solution)/shard_map/all_gather | solution.py:34
  167.9 4.7 fusion.28
  172.6 0.7 pad_maximum_fusion
  173.4 0.0 all-gather.9.cloned.1.call-update
  173.4 0.0 all-gather.11.cloned.1.call-start
  173.4 0.7 all-gather.11.cloned.1.call-update
  174.1 0.0 reduce-scatter.3.cloned.1.call-start
  174.2 120.9 %all-gather.9.cloned.1.call-done = bf16[4096,512]{0,1:T(8,128)(2,1)} async-done(((bf16[256,512]{0,1:T(8,128)(2,1)}), bf16[4096,512]{0,1:T(8,128)(2,1)}) %all-gather.9.cloned.1.call-update) | async-done | bytes 4194320 | tf_op jit(solution)/shard_map/all_gather | solution.py:77
  295.1 2.7 fusion.113
  297.8 1.4 multiply_reduce_fusion
  299.3 1.5 fusion
  300.8 1.8 fusion.37
  302.6 0.0 copy-start.2
  302.6 69.4 %all-gather.11.cloned.1.call-done = bf16[4096,256]{1,0:T(8,128)(2,1)} async-done(((bf16[256,256]{1,0:T(8,128)(2,1)}), bf16[4096,256]{1,0:T(8,128)(2,1)}) %all-gather.11.cloned.1.call-update) | async-done | bytes 2097168 | tf_op jit(solution)/shard_map/all_gather | solution.py:42
  372.0 3.7 convolution_convert_fusion.1
  375.7 0.0 reduce-scatter.3.cloned.1.call-update
  375.7 0.0 all-gather.13.cloned.1.call-start
  375.8 77.6 %reduce-scatter.3.cloned.1.call-done = bf16[256,256]{1,0:T(8,128)(2,1)} async-done(((bf16[256,4096]{1,0:T(8,128)(2,1)}), bf16[256,256]{1,0:T(8,128)(2,1)}) %reduce-scatter.3.cloned.1.call-update) | async-done | bytes 131088 | tf_op jit(solution)/shard_map/reduce_scatter | solution.py:49
  453.4 1.6 add_convert_fusion.1
  455.0 0.0 all-gather.13.cloned.1.call-update
  455.0 0.0 all-gather.15.cloned.1.call-start
  455.1 0.5 all-gather.15.cloned.1.call-update
  455.6 0.0 all-gather.17.cloned.1.call-start
  455.7 0.7 all-gather.17.cloned.1.call-update
  456.4 0.0 reduce-scatter.5.cloned.1.call-start
  456.5 50.9 %all-gather.13.cloned.1.call-done = bf16[256,4096]{1,0:T(8,128)(2,1)} async-done(((bf16[256,256]{1,0:T(8,128)(2,1)}), bf16[256,4096]{1,0:T(8,128)(2,1)}) %all-gather.13.cloned.1.call-update) | async-done | bytes 2097168 | tf_op jit(solution)/shard_map/all_gather | solution.py:108
  507.3 2.1 convert_reduce_fusion
  509.4 2.3 fusion.6
  511.7 0.0 copy-start.5
  511.7 0.0 copy-start.6
  511.7 94.5 %all-gather.15.cloned.1.call-done = bf16[2,4096,256]{2,1,0:T(8,128)(2,1)} async-done(((bf16[2,256,256]{2,1,0:T(8,128)(2,1)}), bf16[2,4096,256]{2,1,0:T(8,128)(2,1)}) %all-gather.15.cloned.1.call-update) | async-done | bytes 4194320 | tf_op jit(solution)/shard_map/all_gather | solution.py:34
  606.3 3.5 fusion.20
  609.8 0.1 fusion.76
  609.9 3.8 collective-permute-start
  613.7 2.9 collective-permute-start.1
  616.6 0.1 fusion.125
  616.7 0.0 collective-permute-done
  616.7 2.5 collective-permute-done.1
  619.3 61.2 %all-gather.17.cloned.1.call-done = bf16[4096,256]{1,0:T(8,128)(2,1)} async-done(((bf16[256,256]{1,0:T(8,128)(2,1)}), bf16[4096,256]{1,0:T(8,128)(2,1)}) %all-gather.17.cloned.1.call-update) | async-done | bytes 2097168 | tf_op jit(solution)/shard_map/all_gather | solution.py:42
  680.5 4.6 convolution_convert_fusion
  685.1 0.0 reduce-scatter.5.cloned.1.call-update
  685.1 77.9 %reduce-scatter.5.cloned.1.call-done = bf16[256,256]{1,0:T(8,128)(2,1)} async-done(((bf16[256,4096]{1,0:T(8,128)(2,1)}), bf16[256,256]{1,0:T(8,128)(2,1)}) %reduce-scatter.5.cloned.1.call-update) | async-done | bytes 131088 | tf_op jit(solution)/shard_map/reduce_scatter | solution.py:49
  763.0 1.6 add_convert_fusion
  (22 shorter events, 0.2 us)
Async XLA Ops:
  6.5 4.1 copy-start
  6.5 161.3 %copy-start.3 = (f32[4096]{0:T(1024)S(1)}, f32[4096]{0:T(1024)}, u32[]{:S(2)}) copy-start(f32[4096]{0:T(1024)} %param.11) | copy-start | bytes 49156
  6.5 161.3 %all-gather.7.cloned.1.call-start = ((), (), s32[]{:S(2)}) async-start(), calls=%async_computation.2 | async-start | bytes 6684672 | tf_op jit(solution)/shard_map/all_gather | solution.py:34
  8.6 286.5 %all-gather.9.cloned.1.call-start = ((), (), s32[]{:S(2)}) async-start(), calls=%async_computation.3 | async-start | bytes 4456448 | tf_op jit(solution)/shard_map/all_gather | solution.py:77
  173.4 198.6 %all-gather.11.cloned.1.call-start = ((), (), s32[]{:S(2)}) async-start(), calls=%async_computation.4 | async-start | bytes 2228224 | tf_op jit(solution)/shard_map/all_gather | solution.py:42
  174.1 279.3 %reduce-scatter.3.cloned.1.call-start = ((), (), s32[]{:S(2)}) async-start(), calls=%async_computation.5 | async-start | bytes 2228224 | tf_op jit(solution)/shard_map/reduce_scatter | solution.py:49
  302.6 153.8 %copy-start.2 = (f32[31,256]{1,0:T(8,128)S(1)}, f32[31,256]{1,0:T(8,128)}, u32[]{:S(2)}) copy-start(f32[31,256]{1,0:T(8,128)} %param.16) | copy-start | bytes 95236
  375.7 230.6 %copy-start.4 = (f32[4096]{0:T(1024)S(1)}, f32[4096]{0:T(1024)}, u32[]{:S(2)}) copy-start(f32[4096]{0:T(1024)} %param.14) | copy-start | bytes 49156
  375.7 131.6 %all-gather.13.cloned.1.call-start = ((), (), s32[]{:S(2)}) async-start(), calls=%async_computation.6 | async-start | bytes 2228224 | tf_op jit(solution)/shard_map/all_gather | solution.py:108
  455.0 151.2 %all-gather.15.cloned.1.call-start = ((), (), s32[]{:S(2)}) async-start(), calls=%async_computation.7 | async-start | bytes 4456448 | tf_op jit(solution)/shard_map/all_gather | solution.py:34
  455.6 224.9 %all-gather.17.cloned.1.call-start = ((), (), s32[]{:S(2)}) async-start(), calls=%async_computation.8 | async-start | bytes 2228224 | tf_op jit(solution)/shard_map/all_gather | solution.py:42
  456.4 306.7 %reduce-scatter.5.cloned.1.call-start = ((), (), s32[]{:S(2)}) async-start(), calls=%async_computation.9 | async-start | bytes 2228224 | tf_op jit(solution)/shard_map/reduce_scatter | solution.py:49
  507.3 99.0 %copy-start.1 = (bf16[256,4096]{1,0:T(8,128)(2,1)S(1)}, bf16[256,4096]{1,0:T(8,128)(2,1)}, u32[]{:S(2)}) copy-start(bf16[256,4096]{1,0:T(8,128)(2,1)} %all-gather.13.cloned.1.call-done) | copy-start | bytes 6291460
  511.7 168.8 %copy-start.5 = (f32[256]{0:T(256)S(1)}, f32[256]{0:T(256)}, u32[]{:S(2)}) copy-start(f32[256]{0:T(256)} %param.18) | copy-start | bytes 3076
  511.7 168.8 %copy-start.6 = (f32[256]{0:T(256)S(1)}, f32[256]{0:T(256)}, u32[]{:S(2)}) copy-start(f32[256]{0:T(256)} %param.17) | copy-start | bytes 3076
  609.9 6.8 collective-permute-start
  613.7 5.5 collective-permute-start.1
Sparse Core Ops, SparseCore 0:
  9.1 158.7 all-gather.6
  173.5 121.5 all-gather.8
  296.9 75.0 all-gather.10
  376.1 77.3 reduce-scatter.2
  456.1 51.1 all-gather.12
  509.1 97.1 all-gather.14
  608.2 72.2 all-gather.16
  685.3 77.7 reduce-scatter.4
